TPU v7x, 32 devices: a whole 2x2x4 slice. The times are simulated.
32 devices in a mesh: groups: 2 (over y), tensor: 8 (over z, x), replica: 2 (over core).
Axes of the slice: x: 2, y: 2, z: 4, core: 2. Of those that a mesh axis runs over, the one named last changes fastest.
Arguments:
- activations: bfloat16 [2, 1024, 8192], P(None, ('groups', 'replica'), 'tensor'), parts along dimension 1, may hold values from -6 to 6
- request_adapter_index: int32 [2, 1024], P(None, 'groups'), parts along dimension 1, may hold values from 0 to 47
- adapter_pool_row: int32 [48], replicated, may hold values from 0 to 47, each once
- gate_weight_matrix: bfloat16 [8192, 28672], P(None, 'tensor'), may hold values from -0.0625 to 0.0625
- adapter_down_factors: bfloat16 [48, 8192, 64], P('replica', 'tensor'), may hold values from -0.0625 to 0.0625
- adapter_up_factors: bfloat16 [48, 64, 28672], P('replica', None, 'tensor'), may hold values from -0.75 to 0.75
Outputs:
- projected: bfloat16 [2, 1024, 28672], P(None, ('groups', 'replica'), 'tensor'), parts along dimension 1
There are 2 independent parts, one for each index of `groups`. A program takes and returns all parts, laid end to end along the dimension named above; an argument that names none is the same for every part. Nothing has to cross between parts.
Inputs may be any that keep to these rules, and one draw needn't show every extreme that they name: `adapter_pool_row`: pool rows r * 24 to (r + 1) * 24 - 1 are those placed on index r of replica; each adapter has one pool row. `request_adapter_index`: each entry names an adapter.
All inputs are finite; a program needn't handle non-finite values.
Results may differ from a plain program's by a relative error of at most 0.0065.
Values may be sent and summed in bfloat16 or wider, within the bound.
A program may use at most 256 MiB of HBM per device.

v0:
```python
import jax
import jax.numpy as jnp
from jax import lax
from jax.sharding import PartitionSpec as P


def swapped(value, axis, bit):
    return lax.ppermute(value, axis, [(i, i ^ 1 << bit) for i in range(lax.axis_size(axis))])


def pool_rows(row_ids, adapter_pool_row):
    table = jnp.arange(adapter_pool_row.shape[0], dtype=jnp.int32)
    matches = row_ids[:, None] == table[None, :]
    return jnp.sum(jnp.where(matches, adapter_pool_row[None, :], 0), axis=1)


def adapter_delta(row_inputs, local_slots, down_pool, up_pool):
    held = down_pool.shape[0]
    owned = local_slots[:, None] == jnp.arange(held, dtype=jnp.int32)[None, :]
    partial_all = jnp.einsum(
        "nd,adr->nar", row_inputs, down_pool, preferred_element_type=jnp.float32
    )
    partial_value = jnp.sum(jnp.where(owned[:, :, None], partial_all, 0.0), axis=1)
    shrunk_inputs = lax.psum(partial_value, "tensor").astype(jnp.bfloat16)
    spread = jnp.where(
        owned[:, :, None], shrunk_inputs[:, None, :], jnp.zeros_like(shrunk_inputs)[:, None, :]
    )
    spread = spread.reshape(spread.shape[0], held * spread.shape[2])
    flat_up = up_pool.reshape(held * up_pool.shape[1], up_pool.shape[2])
    return jnp.dot(spread, flat_up, preferred_element_type=jnp.float32).astype(jnp.bfloat16)


def on_device(
    activations,
    request_adapter_index,
    adapter_pool_row,
    gate_weight_matrix,
    adapter_down_factors,
    adapter_up_factors,
):
    replica_index = lax.axis_index("replica")
    rows_dev = activations.shape[1]
    held = adapter_down_factors.shape[0]
    own_ids = lax.dynamic_slice_in_dim(request_adapter_index, replica_index * rows_dev, rows_dev, 1)
    other_ids = lax.dynamic_slice_in_dim(
        request_adapter_index, (1 - replica_index) * rows_dev, rows_dev, 1
    )
    partner_inputs = swapped(activations, "replica", 0)
    steps_total = activations.shape[0]
    results = []
    for step_index in range(steps_total):
        own_inputs = activations[step_index]
        base = jnp.dot(
            lax.all_gather(own_inputs, "tensor", axis=1, tiled=True),
            gate_weight_matrix,
            preferred_element_type=jnp.float32,
        )
        own_slots = pool_rows(own_ids[step_index], adapter_pool_row)
        count = own_inputs.shape[0]
        both_inputs = jnp.concatenate([own_inputs, partner_inputs[step_index]], axis=0)
        both_slots = (
            jnp.concatenate([own_slots, pool_rows(other_ids[step_index], adapter_pool_row)], axis=0)
            - replica_index * held
        )
        both_delta = adapter_delta(
            both_inputs, both_slots, adapter_down_factors, adapter_up_factors
        )
        returned = swapped(both_delta[count:], "replica", 0)
        delta = both_delta[:count].astype(jnp.float32) + returned.astype(jnp.float32)
        results.append((base + delta).astype(jnp.bfloat16))
    return jnp.stack(results)


def solution(mesh):
    return jax.shard_map(
        on_device,
        mesh=mesh,
        in_specs=(
            P(None, ("groups", "replica"), "tensor"),
            P(None, "groups"),
            P(),
            P(None, "tensor"),
            P("replica", "tensor", None),
            P("replica", None, "tensor"),
        ),
        out_specs=P(None, ("groups", "replica"), "tensor"),
        check_vma=False,
    )
```

profile of v0, /device:TPU:0, one launch (start us, length us, event | category | flops | bytes accessed | tf_op | source)
XLA Modules:
  0.0 203.4 jit_solution(11583975284465155544)
XLA Ops:
  6.5 2.8 %fusion.26 = (bf16[1,256,1024]{2,1,0:T(8,128)(2,1)}, bf16[256,1024]{1,0:T(8,128)(2,1)}, bf16[256,1024]{1,0:T(8,128)(2,1)}, bf16[1,256,1024]{2,1,0:T(8,128)(2,1)}) fusion(bf16[2,256,1024]{2,1,0:T(8,128)(2,1)} %param.6), kind=kLoop, calls=%fused_computation.51 | loop fusion | bytes 3145728 | tf_op jit(solution)/shard_map/slice | solution.py:52
  9.4 0.5 collective-permute-start
  9.9 0.2 all-gather.7.cloned.1.call-update
  10.2 0.1 fusion.27
  10.2 0.1 select_reduce_fusion.5
  10.4 2.2 %collective-permute-done = bf16[2,256,1024]{2,1,0:T(8,128)(2,1)} collective-permute-done((bf16[2,256,1024]{2,1,0:T(8,128)(2,1)}, bf16[2,256,1024]{2,1,0:T(8,128)(2,1)}, u32[]{:S(2)}, u32[]{:S(2)}) %collective-permute-start) | collective-permute-done | bytes 1048608 | tf_op jit(solution)/shard_map/ppermute | solution.py:8
  12.6 1.3 slice_bitcast_fusion.1
  13.9 2.9 %fusion.10 = f32[512,1536]{0,1:S(1)} fusion(bf16[1024,1536]{0,1:T(8,128)(2,1)S(1)} %bitcast.43, bf16[256,1024]{1,0:T(8,128)(2,1)S(1)} %get-tuple-element.15, bf16[256,1024]{1,0:T(8,128)(2,1)} %get-tuple-element.12), kind=kOutput, calls=%fused_computation.17 | convolution fusion | flops 1612709888 | bytes 7340032
  16.8 0.4 select_reduce_fusion.1
  17.2 0.6 copy-done.4
  17.8 1.8 fusion.14
  19.7 0.4 select_reduce_fusion
  20.1 45.8 %all-reduce.2 = (bf16[512,64]{0,1:T(8,128)(2,1)S(1)}, bf16[512,64]{0,1:T(8,128)(2,1)S(1)}) all-reduce(f32[512,64]{0,1:T(8,128)S(1)} %select_reduce_fusion, f32[512,64]{0,1:T(8,128)S(1)} %select_reduce_fusion.1), channel_id=1, replica_groups=mesh['groups'=2,'tensor'=8,'replica'=2] {'tensor'}, use_global_device_ids=true, to_apply=%region_7.8 | all-reduce | flops 65536 | bytes 393216 | tf_op jit(solution)/shard_map/psum | solution.py:24
  65.9 10.3 %bitcast_convert_fusion.1 = bf16[512,3584]{1,0:T(8,128)(2,1)S(1)} fusion(bf16[24,64,3584]{2,1,0:T(8,128)(2,1)} %param.11, pred[512,24]{0,1:T(8,128)(4,1)S(1)} %iota_compare_fusion.3, bf16[512,64]{0,1:T(8,128)(2,1)S(1)} %get-tuple-element.10), kind=kOutput, calls=%fused_computation.1 | convolution fusion | flops 5639766016 | bytes 14757888 | tf_op jit(solution)/shard_map/dot_general | solution.py:30
  76.2 0.1 slice.50
  76.4 1.6 copy-done.3
  78.0 10.3 %bitcast_convert_fusion = bf16[512,3584]{1,0:T(8,128)(2,1)S(1)} fusion(bf16[24,64,3584]{2,1,0:T(8,128)(2,1)} %param.11, pred[512,24]{0,1:T(8,128)(4,1)S(1)} %iota_compare_fusion, bf16[512,64]{0,1:T(8,128)(2,1)S(1)} %get-tuple-element.9), kind=kOutput, calls=%fused_computation | convolution fusion | flops 5639766016 | bytes 14757888 | tf_op jit(solution)/shard_map/dot_general | solution.py:30
  88.3 0.1 slice.53
  88.4 0.1 collective-permute-start.2
  88.5 1.6 copy-done.2
  90.1 27.6 %fusion.4 = bf16[1,256,3584]{2,1,0:T(8,128)(2,1)} fusion(bf16[256,3584]{1,0:T(8,128)(2,1)} %collective-permute-done.1, bf16[512,3584]{1,0:T(8,128)(2,1)} %copy-done.3, bf16[8192,3584]{1,0:T(8,128)(2,1)} %param.9, bf16[1,256,8192]{2,1,0:T(8,128)(2,1)} %all-gather.5.cloned.1.call-done), kind=kOutput, calls=%fused_computation.11 | convolution fusion | flops 15036973056 | bytes 68419584 | tf_op jit(solution)/shard_map/dot_general | solution.py:53
  117.7 47.5 %all-gather.7.cloned.1.call-done = bf16[1,256,8192]{2,1,0:T(8,128)(2,1)} async-done(((bf16[1,256,1024]{2,1,0:T(8,128)(2,1)}), bf16[1,256,8192]{2,1,0:T(8,128)(2,1)}) %all-gather.7.cloned.1.call-update) | async-done | bytes 4194320 | tf_op jit(solution)/shard_map/all_gather | solution.py:54
  165.2 27.1 %fusion.5 = bf16[1,256,3584]{2,1,0:T(8,128)(2,1)} fusion(bf16[256,3584]{1,0:T(8,128)(2,1)} %collective-permute-done.2, bf16[512,3584]{1,0:T(8,128)(2,1)} %copy-done.2, bf16[8192,3584]{1,0:T(8,128)(2,1)} %param.9, bf16[1,256,8192]{2,1,0:T(8,128)(2,1)} %all-gather.7.cloned.1.call-done), kind=kOutput, calls=%fused_computation.12 | convolution fusion | flops 15036973056 | bytes 68419584 | tf_op jit(solution)/shard_map/dot_general | solution.py:53
  192.3 4.2 %pad_maximum_fusion = bf16[2,256,3584]{2,1,0:T(8,128)(2,1)} fusion(bf16[1,256,3584]{2,1,0:T(8,128)(2,1)} %fusion.5, bf16[1,256,3584]{2,1,0:T(8,128)(2,1)} %fusion.4), kind=kLoop, calls=%fused_computation.6 | loop fusion | flops 1835008 | bytes 7340032 | tf_op jit(solution)/shard_map/stack | solution.py:71
  (21 shorter events, 0.2 us)
Async XLA Ops:
  6.5 7.3 %copy-start = (bf16[24,1024,64]{1,2,0:T(8,128)(2,1)S(1)}, bf16[24,1024,64]{1,2,0:T(8,128)(2,1)}, u32[]{:S(2)}) copy-start(bf16[24,1024,64]{1,2,0:T(8,128)(2,1)} %param.10) | copy-start | bytes 9437188
  6.5 3.6 %copy-start.5 = (s32[2,512]{1,0:T(2,128)S(1)}, s32[2,512]{1,0:T(2,128)}, u32[]{:S(2)}) copy-start(s32[2,512]{1,0:T(2,128)} %param.7) | copy-start | bytes 12292
  6.5 3.7 %copy-start.6 = (s32[48]{0:T(128)S(1)}, s32[48]{0:T(128)}, u32[]{:S(2)}) copy-start(s32[48]{0:T(128)} %param.8) | copy-start | bytes 580
  6.5 83.6 %all-gather.5.cloned.1.call-start = ((), (), s32[]{:S(2)}) async-start(), calls=%async_computation | async-start | bytes 4718592 | tf_op jit(solution)/shard_map/all_gather | solution.py:54
  9.4 155.9 %all-gather.7.cloned.1.call-start = ((), (), s32[]{:S(2)}) async-start(), calls=%async_computation.1 | async-start | bytes 4718592 | tf_op jit(solution)/shard_map/all_gather | solution.py:54
  9.4 3.1 %collective-permute-start = (bf16[2,256,1024]{2,1,0:T(8,128)(2,1)}, bf16[2,256,1024]{2,1,0:T(8,128)(2,1)}, u32[]{:S(2)}, u32[]{:S(2)}) collective-permute-start(bf16[2,256,1024]{2,1,0:T(8,128)(2,1)} %param.6), channel_id=1, source_target_pairs={{0,1},{1,0},{2,3},{3,2},{4,5},{5,4},{6,7},{7,6},{8,9},{9,8},{10,11... | collective-permute-start | bytes 3145736 | tf_op jit(solution)/shard_map/ppermute | solution.py:8
  16.8 1.0 copy-start.4
  76.2 1.8 copy-start.3
  76.3 13.8 %collective-permute-start.1 = (bf16[256,3584]{1,0:T(8,128)(2,1)S(1)}, bf16[256,3584]{1,0:T(8,128)(2,1)}, u32[]{:S(2)}, u32[]{:S(2)}) collective-permute-start(bf16[256,3584]{1,0:T(8,128)(2,1)S(1)} %slice.50), channel_id=1, source_target_pairs={{0,1},{1,0},{2,3},{3,2},{4,5},{5,4},{6,7},{7,6},{8,9},{9,8},{10,11... | collective-permute-start | bytes 5505032 | tf_op jit(solution)/shard_map/ppermute | solution.py:8
  88.3 1.8 copy-start.2
  88.4 29.3 %collective-permute-start.2 = (bf16[256,3584]{1,0:T(8,128)(2,1)S(1)}, bf16[256,3584]{1,0:T(8,128)(2,1)}, u32[]{:S(2)}, u32[]{:S(2)}) collective-permute-start(bf16[256,3584]{1,0:T(8,128)(2,1)S(1)} %slice.53), channel_id=1, source_target_pairs={{0,1},{1,0},{2,3},{3,2},{4,5},{5,4},{6,7},{7,6},{8,9},{9,8},{10,11... | collective-permute-start | bytes 5505032 | tf_op jit(solution)/shard_map/ppermute | solution.py:8
  165.2 31.3 %copy-start.1 = (bf16[24,1024,64]{1,2,0:T(8,128)(2,1)S(1)}, bf16[24,1024,64]{1,2,0:T(8,128)(2,1)}, u32[]{:S(2)}) copy-start(bf16[24,1024,64]{1,2,0:T(8,128)(2,1)} %param.10) | copy-start | bytes 9437188
Sparse Core Ops, SparseCore 0:
  9.5 80.2 all-gather.4
  92.0 73.1 all-gather.6
where the time goes:
time: 204 us; the launch traced here: 203 us
  matrix products  80 us (39%)
  waiting for transfers between devices  49.9 us (24%)
  blocking collectives  45.8 us (22%)
  between operations  13.6 us (7%)
  local copies, waits for them, and re-layouts  8.26 us (4%)
  other arithmetic  5.23 us (3%)
    dot_general x2, matrix products, on_device(): jnp.dot(lax.all_gather(own_inputs, 'tensor', axis=1, tiled=True), gate_we...  54.7 us
    all_gather x2, waiting for transfers between devices, on_device(): lax.all_gather(own_inputs, 'tensor', axis=1, tiled=True)  47.5 us
    psum x1, blocking collectives, adapter_delta(): shrunk_inputs = lax.psum(partial_value, 'tensor').astype(jnp.bfloat16)  45.8 us
    dot_general x2, matrix products, adapter_delta(): jnp.dot(spread, flat_up, preferred_element_type=jnp.float32)  20.5 us
    unnamed x2, matrix products  4.74 us
    another operation x1, other arithmetic, on_device(): return jnp.stack(results)  4.22 us
  transfers between devices with their start and end apart: 5, of which 2 were waited for; matrix products, arithmetic and copies ran while one was open for 27% of the time, Pallas kernels for 0%

commit v1 on v0

--- a/solution.py
+++ b/solution.py
@@ -1,7 +1,433 @@
 import jax
 import jax.numpy as jnp
 from jax import lax
+from jax.experimental import pallas as pl
+from jax.experimental.pallas import tpu as pltpu
 from jax.sharding import PartitionSpec as P
+
+MESH = pl.DeviceIdType.MESH
+TILE = 512
+LINK_X, LINK_A, LINK_B = 0, 1, 2
+
+
+def fused_kernel(
+    act, slots, down, gate, up, out,
+    xg, acc, wbuf, upbuf, downbuf, spread, dsend, drecv, px, pk, rsbuf, agbuf,
+    xsend, xrecv, wsem, upsem, insem, pxsem, dsem, rs_send, rs_recv, ag_send, ag_recv, osem,
+):
+    total = lax.axis_size("tensor")
+    me = lax.axis_index("tensor")
+    replica = lax.axis_index("replica")
+    steps, rows, feats = act.shape
+    tiles = out.shape[2] // TILE
+    lanes = pk.shape[2]
+    rank = lanes // 2
+    block = pk.shape[1]
+    held = downbuf.shape[0] // rank
+
+    z, x = me // 2, me % 2
+    far = z // 2
+    zz = z + far * (3 - 2 * z)
+
+    def own_col(k):
+        return (k + far * (3 - 2 * k)) * 2 + x
+
+    def other_col(k):
+        return (k + far * (3 - 2 * k)) * 2 + 1 - x
+
+    own = [own_col(k) for k in range(4)]
+    other = [other_col(k) for k in range(4)]
+    corner = [own[0], other[0], own[1], own[2], other[2], own[3], other[1], other[3]]
+    middle = [own[1], other[1], own[0], own[2], own[3], other[0], other[2], other[3]]
+    order = [zz * m + (1 - zz) * c for c, m in zip(corner, middle)]
+
+    act_copy = pltpu.make_async_copy(act, xg.at[me], insem.at[0])
+    act_copy.start()
+    down_copy = pltpu.make_async_copy(down, downbuf, insem.at[1])
+    down_copy.start()
+
+    mate = z * 2 + 1 - x
+
+    def weights(i):
+        start = pl.multiple_of(order[i] * feats, feats)
+        return pltpu.make_async_copy(gate.at[pl.ds(start, feats), :], wbuf.at[i % 2], wsem.at[i % 2])
+
+    def up_tile(n):
+        cols = pl.ds(pl.multiple_of(n * TILE, TILE), TILE)
+        return pltpu.make_async_copy(up.at[:, cols], upbuf.at[n % 2], upsem.at[n % 2])
+
+    weights(0).start()
+    up_tile(0).start()
+
+    barrier = pltpu.get_barrier_semaphore()
+    for d in range(1, total):
+        pl.semaphore_signal(barrier, inc=1, device_id={"tensor": (me + d) % total}, device_id_type=MESH)
+    pl.semaphore_signal(barrier, inc=1, device_id={"replica": 1 - replica}, device_id_type=MESH)
+    pl.semaphore_wait(barrier, total)
+
+    def piece(slot, half, link, target):
+        return pltpu.make_async_remote_copy(
+            src_ref=xg.at[slot, half], dst_ref=xg.at[slot, half],
+            send_sem=xsend.at[link, slot, half], recv_sem=xrecv.at[slot, half],
+            device_id={"tensor": target}, device_id_type=MESH)
+
+    def arrived(slot, half):
+        piece(slot, half, LINK_X, mate).wait_recv()
+
+    corner_next = own[1]
+    middle_edge, middle_inner = own[0], own[2]
+    corner_sends = []
+    middle_sends = []
+
+    def corner_send(slot, half, link):
+        corner_sends.append((slot, half, link))
+        piece(slot, half, link, mate if link == LINK_X else corner_next).start()
+
+    def middle_send(slot, half, link):
+        middle_sends.append((slot, half, link))
+        piece(slot, half, link, (mate, middle_edge, middle_inner)[link]).start()
+
+    act_copy.wait()
+    swap = pltpu.make_async_remote_copy(
+        src_ref=xg.at[me], dst_ref=px, send_sem=pxsem.at[0], recv_sem=pxsem.at[1],
+        device_id={"replica": 1 - replica}, device_id_type=MESH)
+    swap.start()
+
+    @pl.when(zz == 0)
+    def _():
+        for half in range(2):
+            corner_send(own[0], half, LINK_X)
+            corner_send(own[0], half, LINK_A)
+
+    @pl.when(zz == 1)
+    def _():
+        for half in range(2):
+            middle_send(own[1], half, LINK_X)
+            middle_send(own[1], half, LINK_A)
+            middle_send(own[1], half, LINK_B)
+
+    weights(1).start()
+
+    low_lanes = lax.broadcasted_iota(jnp.int32, (rows, lanes), 1) < rank
+    lane_half = (lax.broadcasted_iota(jnp.int32, (rows, lanes), 1) >= rank).astype(jnp.int32)
+
+    def partial_shrink(inputs, step, group):
+        slot = slots[step, group * rows:(group + 1) * rows, :]
+        wanted = jnp.broadcast_to(slot, (rows, lanes)) - lane_half
+        found = jnp.zeros((rows, lanes), jnp.float32)
+        wide = 2 * lanes
+        for t in range(held * rank // wide):
+            product = lax.dot_general(
+                inputs, downbuf[t * wide:(t + 1) * wide, :], (((1,), (1,)), ((), ())),
+                preferred_element_type=jnp.float32)
+            for part in range(2):
+                first = (t * 2 + part) * 2
+                found = found + jnp.where(wanted == first, product[:, part * lanes:(part + 1) * lanes], 0.0)
+        return found + pltpu.roll(found, rank, 1)
+
+    down_copy.wait()
+    half_blocks = total // 2
+    for group in range(2):
+        if group == 1:
+            swap.wait()
+        pair = [
+            partial_shrink(px[step] if group else xg[me, step], step, group) for step in range(2)
+        ]
+        packed = jnp.where(low_lanes, pair[0], pair[1])
+        pk[group * half_blocks:(group + 1) * half_blocks] = packed.reshape(half_blocks, block, lanes)
+
+    def reduce_copy(d):
+        return pltpu.make_async_remote_copy(
+            src_ref=pk.at[(me + d) % total], dst_ref=rsbuf.at[me],
+            send_sem=rs_send.at[d], recv_sem=rs_recv.at[d],
+            device_id={"tensor": (me + d) % total}, device_id_type=MESH)
+
+    def reduce_arrival(d):
+        source = (me + total - d) % total
+        return pltpu.make_async_remote_copy(
+            src_ref=pk.at[source], dst_ref=rsbuf.at[source],
+            send_sem=rs_send.at[d], recv_sem=rs_recv.at[d],
+            device_id={"tensor": source}, device_id_type=MESH)
+
+    def gather_copy(d):
+        return pltpu.make_async_remote_copy(
+            src_ref=agbuf.at[me], dst_ref=agbuf.at[me],
+            send_sem=ag_send.at[d], recv_sem=ag_recv.at[d],
+            device_id={"tensor": (me + d) % total}, device_id_type=MESH)
+
+    def gather_arrival(d):
+        source = (me + total - d) % total
+        return pltpu.make_async_remote_copy(
+            src_ref=agbuf.at[source], dst_ref=agbuf.at[source],
+            send_sem=ag_send.at[d], recv_sem=ag_recv.at[d],
+            device_id={"tensor": source}, device_id_type=MESH)
+
+    for d in range(1, total):
+        reduce_copy(d).start()
+
+    def multiply(i):
+        weights(i).wait()
+
+        def body(n, carry):
+            cols = pl.ds(pl.multiple_of(n * TILE, TILE), TILE)
+            product = jnp.dot(
+                xg[order[i]].reshape(steps * rows, feats), wbuf[i % 2, :, cols],
+                preferred_element_type=jnp.float32)
+            if i == 0:
+                acc[n] = product
+            else:
+                acc[n] += product
+            return carry
+
+        lax.fori_loop(0, tiles, body, 0)
+        if i + 2 < total:
+            weights(i + 2).start()
+
+    multiply(0)
+
+    for d in range(1, total):
+        reduce_arrival(d).wait_recv()
+    summed = pk[me]
+    for d in range(1, total):
+        summed = summed + rsbuf[(me + total - d) % total]
+    agbuf[me] = summed.astype(jnp.bfloat16)
+    for d in range(1, total):
+        gather_copy(d).start()
+
+    @pl.when(zz == 0)
+    def _():
+        arrived(own[1], 0)
+        corner_send(own[1], 0, LINK_X)
+
+    @pl.when(zz == 1)
+    def _():
+        arrived(own[2], 0)
+        middle_send(own[2], 0, LINK_A)
+        middle_send(own[2], 0, LINK_X)
+        arrived(own[0], 0)
+        middle_send(own[0], 0, LINK_X)
+        middle_send(own[0], 0, LINK_B)
+
+    for d in range(1, total):
+        gather_arrival(d).wait_recv()
+
+    def fill_spread(group):
+        packed = agbuf[group * half_blocks:(group + 1) * half_blocks].reshape(rows, lanes).astype(jnp.float32)
+        turned = pltpu.roll(packed, rank, 1)
+        for step in range(2):
+            both = jnp.where(low_lanes, packed, turned) if step == 0 else jnp.where(low_lanes, turned, packed)
+            slot = slots[step, group * rows:(group + 1) * rows, :]
+            wanted = jnp.broadcast_to(slot, (rows, lanes)) - lane_half
+            for t in range(held // 2):
+                spread[step * rows:(step + 1) * rows, t * lanes:(t + 1) * lanes] = jnp.where(
+                    wanted == 2 * t, both, 0.0).astype(jnp.bfloat16)
+
+    def expand(group):
+        fill_spread(group)
+
+        def body(n, carry):
+            up_tile(n).wait()
+
+            @pl.when(n + 1 < tiles)
+            def _():
+                up_tile(n + 1).start()
+
+            delta = jnp.dot(spread[...], upbuf[n % 2], preferred_element_type=jnp.float32)
+            if group == 1:
+                dsend[n] = delta.astype(jnp.bfloat16)
+            else:
+                acc[n] += delta
+            return carry
+
+        lax.fori_loop(0, tiles, body, 0)
+
+    expand(1)
+    back = pltpu.make_async_remote_copy(
+        src_ref=dsend, dst_ref=drecv, send_sem=dsem.at[0], recv_sem=dsem.at[1],
+        device_id={"replica": 1 - replica}, device_id_type=MESH)
+    back.start()
+    up_tile(0).start()
+
+    @pl.when(zz == 0)
+    def _():
+        arrived(other[0], 1)
+        corner_send(other[0], 1, LINK_A)
+
+    @pl.when(zz == 1)
+    def _():
+        arrived(own[2], 1)
+        middle_send(own[2], 1, LINK_A)
+        arrived(own[0], 1)
+        middle_send(own[0], 1, LINK_B)
+        arrived(other[1], 1)
+        middle_send(other[1], 1, LINK_B)
+
+    arrived(order[1], 0)
+    multiply(1)
+
+    @pl.when(zz == 0)
+    def _():
+        arrived(own[1], 1)
+
+    multiply(2)
+
+    @pl.when(zz == 0)
+    def _():
+        arrived(own[2], 0)
+        corner_send(own[2], 0, LINK_X)
+
+    @pl.when(zz == 1)
+    def _():
+        arrived(own[3], 0)
+        middle_send(own[3], 0, LINK_A)
+        middle_send(own[3], 0, LINK_X)
+
+    expand(0)
+
+    @pl.when(zz == 0)
+    def _():
+        arrived(own[2], 1)
+        corner_send(own[2], 1, LINK_X)
+
+    @pl.when(zz == 1)
+    def _():
+        arrived(own[3], 1)
+        middle_send(own[3], 1, LINK_A)
+        middle_send(own[3], 1, LINK_X)
+        middle_send(other[1], 1, LINK_A)
+
+    multiply(3)
+
+    @pl.when(zz == 0)
+    def _():
+        arrived(own[3], 0)
+        corner_send(own[3], 0, LINK_X)
+        arrived(other[2], 0)
+        arrived(other[2], 1)
+
+    multiply(4)
+
+    @pl.when(zz == 0)
+    def _():
+        arrived(own[3], 1)
+        corner_send(own[3], 1, LINK_X)
+
+    @pl.when(zz == 1)
+    def _():
+        arrived(other[0], 0)
+        arrived(other[0], 1)
+
+    multiply(5)
+    arrived(order[6], 0)
+    arrived(order[6], 1)
+    multiply(6)
+    back.wait()
+    arrived(order[7], 0)
+    arrived(order[7], 1)
+
+    weights(7).wait()
+
+    def result(n, step):
+        cols = pl.ds(pl.multiple_of(n * TILE, TILE), TILE)
+        return pltpu.make_async_copy(
+            dsend.at[n, pl.ds(step * rows, rows), :], out.at[step, :, cols], osem.at[n, step])
+
+    def finish(n, carry):
+        cols = pl.ds(pl.multiple_of(n * TILE, TILE), TILE)
+        product = jnp.dot(
+            xg[order[7]].reshape(steps * rows, feats), wbuf[1, :, cols],
+            preferred_element_type=jnp.float32)
+        dsend[n] = (acc[n] + product + drecv[n].astype(jnp.float32)).astype(jnp.bfloat16)
+        for step in range(2):
+            result(n, step).start()
+        return carry
+
+    lax.fori_loop(0, tiles, finish, 0)
+
+    @pl.when(zz == 0)
+    def _():
+        for slot, half, link in corner_sends:
+            piece(slot, half, link, mate).wait_send()
+
+    @pl.when(zz == 1)
+    def _():
+        for slot, half, link in middle_sends:
+            piece(slot, half, link, mate).wait_send()
+
+    for d in range(1, total):
+        reduce_copy(d).wait_send()
+        gather_copy(d).wait_send()
+    for n in range(tiles):
+        for step in range(2):
+            result(n, step).wait()
+
+
+def fused(activations, slots, down, gate, up):
+    steps, rows, feats = activations.shape
+    total = lax.axis_size("tensor")
+    columns = gate.shape[1]
+    tiles = columns // TILE
+    rank = up.shape[1]
+    held = up.shape[0]
+    wide = held * rank
+    flops = 2 * steps * rows * columns * (feats * total + 2 * wide)
+    return pl.pallas_call(
+        fused_kernel,
+        out_shape=jax.ShapeDtypeStruct((steps, rows, columns), jnp.bfloat16),
+        in_specs=[
+            pl.BlockSpec(memory_space=pl.ANY),
+            pl.BlockSpec(memory_space=pltpu.VMEM),
+            pl.BlockSpec(memory_space=pl.ANY),
+            pl.BlockSpec(memory_space=pl.ANY),
+            pl.BlockSpec(memory_space=pl.ANY),
+        ],
+        out_specs=pl.BlockSpec(memory_space=pl.ANY),
+        scratch_shapes=[
+            pltpu.VMEM((total, steps, rows, feats), jnp.bfloat16),
+            pltpu.VMEM((tiles, steps * rows, TILE), jnp.float32),
+            pltpu.VMEM((2, feats, columns), jnp.bfloat16),
+            pltpu.VMEM((2, wide, TILE), jnp.bfloat16),
+            pltpu.VMEM((wide, feats), jnp.bfloat16),
+            pltpu.VMEM((steps * rows, wide), jnp.bfloat16),
+            pltpu.VMEM((tiles, steps * rows, TILE), jnp.bfloat16),
+            pltpu.VMEM((tiles, steps * rows, TILE), jnp.bfloat16),
+            pltpu.VMEM((steps, rows, feats), jnp.bfloat16),
+            pltpu.VMEM((total, 2 * rows // total, 2 * rank), jnp.float32),
+            pltpu.VMEM((total, 2 * rows // total, 2 * rank), jnp.float32),
+            pltpu.VMEM((total, 2 * rows // total, 2 * rank), jnp.bfloat16),
+            pltpu.SemaphoreType.DMA((3, total, 2)),
+            pltpu.SemaphoreType.DMA((total, 2)),
+            pltpu.SemaphoreType.DMA((2,)),
+            pltpu.SemaphoreType.DMA((2,)),
+            pltpu.SemaphoreType.DMA((2,)),
+            pltpu.SemaphoreType.DMA((2,)),
+            pltpu.SemaphoreType.DMA((2,)),
+            pltpu.SemaphoreType.DMA((total,)),
+            pltpu.SemaphoreType.DMA((total,)),
+            pltpu.SemaphoreType.DMA((total,)),
+            pltpu.SemaphoreType.DMA((total,)),
+            pltpu.SemaphoreType.DMA((tiles, 2)),
+        ],
+        compiler_params=pltpu.CompilerParams(
+            collective_id=0, has_side_effects=True, vmem_limit_bytes=60 * 1024 * 1024),
+        cost_estimate=pl.CostEstimate(flops=flops, bytes_accessed=80 * 1024 * 1024, transcendentals=0),
+    )(
+        activations, slots,
+        jnp.swapaxes(down, 1, 2).reshape(wide, feats), gate, up.reshape(wide, columns))
+
+
+def on_device_fused(
+    activations, request_adapter_index, adapter_pool_row, gate_weight_matrix, adapter_down_factors, adapter_up_factors
+):
+    replica_index = lax.axis_index("replica")
+    rows_dev = activations.shape[1]
+    held = adapter_down_factors.shape[0]
+    table = jnp.arange(adapter_pool_row.shape[0], dtype=jnp.int32)
+    matches = request_adapter_index[:, :, None] == table
+    slots = jnp.sum(jnp.where(matches, adapter_pool_row, 0), axis=2, keepdims=True) - replica_index * held
+    turned = jnp.concatenate([slots[:, rows_dev:], slots[:, :rows_dev]], axis=1)
+    slots = jnp.where(replica_index == 0, slots, turned)
+    return fused(activations, slots, adapter_down_factors, gate_weight_matrix, adapter_up_factors)
 
 
 def swapped(value, axis, bit):
@@ -72,8 +498,9 @@
 
 
 def solution(mesh):
+    fits = mesh.shape["tensor"] == 8 and mesh.shape["replica"] == 2
     return jax.shard_map(
-        on_device,
+        on_device_fused if fits else on_device,
         mesh=mesh,
         in_specs=(
             P(None, ("groups", "replica"), "tensor"),

time: 204 us -> 119 us (0.58)
  Pallas kernels: 0 us -> 112 us
  matrix products: 80 us -> 0 us
  waiting for transfers between devices: 49.9 us -> 0 us
  blocking collectives: 45.8 us -> 0 us
  between operations: 13.6 us -> 0.05 us
  local copies, waits for them, and re-layouts: 8.26 us -> 4.56 us
  other arithmetic: 5.23 us -> 1.67 us
    pallas_call x0 -> x1, Pallas kernels: none -> 112 us  [fused(): pl.pallas_call(fused_kernel, out_shape=jax.ShapeDtypeStruct((steps, rows,...]
    dot_general x4 -> x0, matrix products: 75.2 us -> none  [the longest x2 54.7 us: on_device(): jnp.dot(lax.all_gather(own_inputs, 'tensor', axis=1, tiled=True), gate_we...]
    all_gather x2 -> x0, waiting for transfers between devices: 47.5 us -> none  [on_device(): lax.all_gather(own_inputs, 'tensor', axis=1, tiled=True)]
    psum x1 -> x0, blocking collectives: 45.8 us -> none  [adapter_delta(): shrunk_inputs = lax.psum(partial_value, 'tensor').astype(jnp.bfloat16)]
    unnamed x2 -> x0, matrix products: 4.74 us -> none
    another operation x1 -> x0, other arithmetic: 4.22 us -> none  [on_device(): return jnp.stack(results)]
    slice x4 -> x1, local copies, waits for them, and re-layouts: 3.13 us -> 0.01 us  [on_device_fused(): turned = jnp.concatenate([slots[:, rows_dev:], slots[:, :rows_dev]], axis=1)]
    ppermute x3 -> x0, waiting for transfers between devices: 2.19 us -> none  [swapped(): lax.ppermute(value, axis, [(i, i ^ 1 << bit) for i in range(lax.axis_size...]
  transfers between devices with their start and end apart: 5 -> 0, of which waited for: 2 -> 0; matrix products, arithmetic and copies ran while one was open for 27% -> 0% of each run, Pallas kernels for 0% -> 0%
where the time goes in v1:
time: 119 us; the launch traced here: 118 us
  Pallas kernels  112 us (94%)
  local copies, waits for them, and re-layouts  4.56 us (4%)
  other arithmetic  1.67 us (1%)
    pallas_call x1, Pallas kernels, fused(): pl.pallas_call(fused_kernel, out_shape=jax.ShapeDtypeStruct((steps, rows,...  112 us
    unnamed x1, local copies, waits for them, and re-layouts  4.11 us

profile of v1, /device:TPU:0, one launch (start us, length us, event | category | flops | bytes accessed | tf_op | source)
XLA Modules:
  0.0 118.3 jit_solution(3994826296106971372)
XLA Ops:
  0.0 0.8 select_reduce_fusion
  0.8 0.2 copy.13
  1.1 0.2 copy.12
  1.3 0.9 broadcast_select_fusion.slots
  2.2 112.0 %shard_map.64 = bf16[2,256,3584]{2,1,0:T(8,128)(2,1)} custom-call(bf16[2,256,1024]{2,1,0:T(8,128)(2,1)} %act.1, s32[2,512,1]{2,1,0:T(8,128)} %broadcast_select_fusion.slots, bf16[1536,1024]{1,0:T(8,128)(2,1)} %bitcast.7, bf16[8192,3584]{1,0:T(8,128)(2,1)} %gate.1, bf16[1536,3584]{1,0:T(8,128)(2,1)} %bitcast.6), custom_call_target="tpu_custom_call" | custom-call | flops 41339060224 | bytes 83886080 | tf_op jit(solution)/shard_map/pallas_call | solution.py:374
  114.2 4.1 %copy.15 = bf16[2,256,3584]{2,1,0:T(8,128)(2,1)} copy(bf16[2,256,3584]{2,1,0:T(8,128)(2,1)} %shard_map.64) | data formatting | bytes 7340032
  (3 shorter events, 0.0 us)

commit v2 on v1

--- a/solution.py
+++ b/solution.py
@@ -6,7 +6,7 @@
 from jax.sharding import PartitionSpec as P
 
 MESH = pl.DeviceIdType.MESH
-TILE = 512
+TILE = 896
 LINK_X, LINK_A, LINK_B = 0, 1, 2
 
 
@@ -93,28 +93,33 @@
         device_id={"replica": 1 - replica}, device_id_type=MESH)
     swap.start()
 
-    @pl.when(zz == 0)
-    def _():
-        for half in range(2):
+    def send_own(half):
+        @pl.when(zz == 0)
+        def _():
             corner_send(own[0], half, LINK_X)
             corner_send(own[0], half, LINK_A)
 
-    @pl.when(zz == 1)
-    def _():
-        for half in range(2):
+        @pl.when(zz == 1)
+        def _():
+            middle_send(own[1], half, LINK_A)
             middle_send(own[1], half, LINK_X)
-            middle_send(own[1], half, LINK_A)
             middle_send(own[1], half, LINK_B)
 
+    send_own(0)
     weights(1).start()
 
+    both_rows = steps * rows
+    half_blocks = total // 2
     low_lanes = lax.broadcasted_iota(jnp.int32, (rows, lanes), 1) < rank
-    lane_half = (lax.broadcasted_iota(jnp.int32, (rows, lanes), 1) >= rank).astype(jnp.int32)
-
-    def partial_shrink(inputs, step, group):
-        slot = slots[step, group * rows:(group + 1) * rows, :]
-        wanted = jnp.broadcast_to(slot, (rows, lanes)) - lane_half
-        found = jnp.zeros((rows, lanes), jnp.float32)
+    lane_half = (lax.broadcasted_iota(jnp.int32, (both_rows, lanes), 1) >= rank).astype(jnp.int32)
+
+    def wanted_first(group):
+        slot = slots[:, group * rows:(group + 1) * rows, :].reshape(both_rows, 1)
+        return jnp.broadcast_to(slot, (both_rows, lanes)) - lane_half
+
+    def partial_shrink(inputs, group):
+        wanted = wanted_first(group)
+        found = jnp.zeros((both_rows, lanes), jnp.float32)
         wide = 2 * lanes
         for t in range(held * rank // wide):
             product = lax.dot_general(
@@ -123,18 +128,15 @@
             for part in range(2):
                 first = (t * 2 + part) * 2
                 found = found + jnp.where(wanted == first, product[:, part * lanes:(part + 1) * lanes], 0.0)
-        return found + pltpu.roll(found, rank, 1)
+        both = found + pltpu.roll(found, rank, 1)
+        packed = jnp.where(low_lanes, both[:rows], both[rows:])
+        pk[group * half_blocks:(group + 1) * half_blocks] = packed.reshape(
+            half_blocks, block, lanes).astype(jnp.bfloat16)
 
     down_copy.wait()
-    half_blocks = total // 2
-    for group in range(2):
-        if group == 1:
-            swap.wait()
-        pair = [
-            partial_shrink(px[step] if group else xg[me, step], step, group) for step in range(2)
-        ]
-        packed = jnp.where(low_lanes, pair[0], pair[1])
-        pk[group * half_blocks:(group + 1) * half_blocks] = packed.reshape(half_blocks, block, lanes)
+    partial_shrink(xg[me].reshape(both_rows, feats), 0)
+    swap.wait()
+    partial_shrink(px[...].reshape(both_rows, feats), 1)
 
     def reduce_copy(d):
         return pltpu.make_async_remote_copy(
@@ -164,6 +166,7 @@
 
     for d in range(1, total):
         reduce_copy(d).start()
+    send_own(1)
 
     def multiply(i):
         weights(i).wait()
@@ -185,15 +188,6 @@
 
     multiply(0)
 
-    for d in range(1, total):
-        reduce_arrival(d).wait_recv()
-    summed = pk[me]
-    for d in range(1, total):
-        summed = summed + rsbuf[(me + total - d) % total]
-    agbuf[me] = summed.astype(jnp.bfloat16)
-    for d in range(1, total):
-        gather_copy(d).start()
-
     @pl.when(zz == 0)
     def _():
         arrived(own[1], 0)
@@ -209,18 +203,22 @@
         middle_send(own[0], 0, LINK_B)
 
     for d in range(1, total):
-        gather_arrival(d).wait_recv()
+        reduce_arrival(d).wait_recv()
+    summed = pk[me].astype(jnp.float32)
+    for d in range(1, total):
+        summed = summed + rsbuf[(me + total - d) % total].astype(jnp.float32)
+    agbuf[me] = summed.astype(jnp.bfloat16)
+    for d in range(1, total):
+        gather_copy(d).start()
 
     def fill_spread(group):
         packed = agbuf[group * half_blocks:(group + 1) * half_blocks].reshape(rows, lanes).astype(jnp.float32)
         turned = pltpu.roll(packed, rank, 1)
-        for step in range(2):
-            both = jnp.where(low_lanes, packed, turned) if step == 0 else jnp.where(low_lanes, turned, packed)
-            slot = slots[step, group * rows:(group + 1) * rows, :]
-            wanted = jnp.broadcast_to(slot, (rows, lanes)) - lane_half
-            for t in range(held // 2):
-                spread[step * rows:(step + 1) * rows, t * lanes:(t + 1) * lanes] = jnp.where(
-                    wanted == 2 * t, both, 0.0).astype(jnp.bfloat16)
+        both = jnp.concatenate(
+            [jnp.where(low_lanes, packed, turned), jnp.where(low_lanes, turned, packed)], axis=0)
+        wanted = wanted_first(group)
+        for t in range(held // 2):
+            spread[:, t * lanes:(t + 1) * lanes] = jnp.where(wanted == 2 * t, both, 0.0).astype(jnp.bfloat16)
 
     def expand(group):
         fill_spread(group)
@@ -241,6 +239,43 @@
 
         lax.fori_loop(0, tiles, body, 0)
 
+    @pl.when(zz == 0)
+    def _():
+        arrived(other[0], 1)
+        corner_send(other[0], 1, LINK_A)
+
+    @pl.when(zz == 1)
+    def _():
+        arrived(own[2], 1)
+        middle_send(own[2], 1, LINK_A)
+        arrived(own[0], 1)
+        middle_send(own[0], 1, LINK_B)
+        arrived(other[1], 1)
+        middle_send(other[1], 1, LINK_B)
+
+    arrived(order[1], 0)
+    multiply(1)
+
+    @pl.when(zz == 0)
+    def _():
+        arrived(own[1], 1)
+
+    multiply(2)
+
+    @pl.when(zz == 0)
+    def _():
+        arrived(own[2], 0)
+        corner_send(own[2], 0, LINK_X)
+
+    @pl.when(zz == 1)
+    def _():
+        arrived(own[3], 0)
+        middle_send(own[3], 0, LINK_A)
+        middle_send(own[3], 0, LINK_X)
+
+    for d in range(1, total):
+        gather_arrival(d).wait_recv()
+
     expand(1)
     back = pltpu.make_async_remote_copy(
         src_ref=dsend, dst_ref=drecv, send_sem=dsem.at[0], recv_sem=dsem.at[1],
@@ -250,42 +285,6 @@
 
     @pl.when(zz == 0)
     def _():
-        arrived(other[0], 1)
-        corner_send(other[0], 1, LINK_A)
-
-    @pl.when(zz == 1)
-    def _():
-        arrived(own[2], 1)
-        middle_send(own[2], 1, LINK_A)
-        arrived(own[0], 1)
-        middle_send(own[0], 1, LINK_B)
-        arrived(other[1], 1)
-        middle_send(other[1], 1, LINK_B)
-
-    arrived(order[1], 0)
-    multiply(1)
-
-    @pl.when(zz == 0)
-    def _():
-        arrived(own[1], 1)
-
-    multiply(2)
-
-    @pl.when(zz == 0)
-    def _():
-        arrived(own[2], 0)
-        corner_send(own[2], 0, LINK_X)
-
-    @pl.when(zz == 1)
-    def _():
-        arrived(own[3], 0)
-        middle_send(own[3], 0, LINK_A)
-        middle_send(own[3], 0, LINK_X)
-
-    expand(0)
-
-    @pl.when(zz == 0)
-    def _():
         arrived(own[2], 1)
         corner_send(own[2], 1, LINK_X)
 
@@ -296,6 +295,8 @@
         middle_send(own[3], 1, LINK_X)
         middle_send(other[1], 1, LINK_A)
 
+    expand(0)
+
     multiply(3)
 
     @pl.when(zz == 0)
@@ -318,31 +319,46 @@
         arrived(other[0], 1)
 
     multiply(5)
-    arrived(order[6], 0)
-    arrived(order[6], 1)
-    multiply(6)
-    back.wait()
-    arrived(order[7], 0)
-    arrived(order[7], 1)
-
-    weights(7).wait()
+    def multiply_half(i, half):
+        part = pl.ds(half * rows, rows)
+
+        def body(n, carry):
+            cols = pl.ds(pl.multiple_of(n * TILE, TILE), TILE)
+            acc[n, part] += jnp.dot(
+                xg[order[i], half], wbuf[i % 2, :, cols], preferred_element_type=jnp.float32)
+            return carry
+
+        lax.fori_loop(0, tiles, body, 0)
 
     def result(n, step):
         cols = pl.ds(pl.multiple_of(n * TILE, TILE), TILE)
         return pltpu.make_async_copy(
             dsend.at[n, pl.ds(step * rows, rows), :], out.at[step, :, cols], osem.at[n, step])
 
-    def finish(n, carry):
-        cols = pl.ds(pl.multiple_of(n * TILE, TILE), TILE)
-        product = jnp.dot(
-            xg[order[7]].reshape(steps * rows, feats), wbuf[1, :, cols],
-            preferred_element_type=jnp.float32)
-        dsend[n] = (acc[n] + product + drecv[n].astype(jnp.float32)).astype(jnp.bfloat16)
-        for step in range(2):
+    def finish(i, step):
+        part = pl.ds(step * rows, rows)
+
+        def body(n, carry):
+            cols = pl.ds(pl.multiple_of(n * TILE, TILE), TILE)
+            product = jnp.dot(
+                xg[order[i], step], wbuf[i % 2, :, cols], preferred_element_type=jnp.float32)
+            dsend[n, part] = (acc[n, part] + product + drecv[n, part].astype(jnp.float32)).astype(jnp.bfloat16)
             result(n, step).start()
-        return carry
-
-    lax.fori_loop(0, tiles, finish, 0)
+            return carry
+
+        lax.fori_loop(0, tiles, body, 0)
+
+    arrived(order[6], 0)
+    weights(6).wait()
+    multiply_half(6, 0)
+    back.wait()
+    arrived(order[7], 0)
+    weights(7).wait()
+    finish(7, 0)
+    arrived(order[6], 1)
+    multiply_half(6, 1)
+    arrived(order[7], 1)
+    finish(7, 1)
 
     @pl.when(zz == 0)
     def _():
@@ -392,8 +408,8 @@
             pltpu.VMEM((tiles, steps * rows, TILE), jnp.bfloat16),
             pltpu.VMEM((tiles, steps * rows, TILE), jnp.bfloat16),
             pltpu.VMEM((steps, rows, feats), jnp.bfloat16),
-            pltpu.VMEM((total, 2 * rows // total, 2 * rank), jnp.float32),
-            pltpu.VMEM((total, 2 * rows // total, 2 * rank), jnp.float32),
+            pltpu.VMEM((total, 2 * rows // total, 2 * rank), jnp.bfloat16),
+            pltpu.VMEM((total, 2 * rows // total, 2 * rank), jnp.bfloat16),
             pltpu.VMEM((total, 2 * rows // total, 2 * rank), jnp.bfloat16),
             pltpu.SemaphoreType.DMA((3, total, 2)),
             pltpu.SemaphoreType.DMA((total, 2)),

time: 119 us -> 106 us (0.89)
  Pallas kernels: 112 us -> 99.4 us
    pallas_call x1, Pallas kernels: 112 us -> 99.4 us  [fused(): pl.pallas_call(fused_kernel, out_shape=jax.ShapeDtypeStruct((steps, rows,...]
where the time goes in v2:
time: 106 us
  Pallas kernels  99.4 us (94%)
  local copies, waits for them, and re-layouts  4.56 us (4%)
  other arithmetic  1.67 us (2%)
    pallas_call x1, Pallas kernels, fused(): pl.pallas_call(fused_kernel, out_shape=jax.ShapeDtypeStruct((steps, rows,...  99.4 us
    unnamed x1, local copies, waits for them, and re-layouts  4.11 us

profile of v2, /device:TPU:0, one launch (start us, length us, event | category | flops | bytes accessed | tf_op | source)
XLA Modules:
  0.0 105.7 jit_solution(18300318749421198191)
XLA Ops:
  0.0 0.8 select_reduce_fusion
  0.8 0.2 copy.13
  1.1 0.2 copy.12
  1.3 0.9 broadcast_select_fusion.slots
  2.2 99.4 %shard_map.64 = bf16[2,256,3584]{2,1,0:T(8,128)(2,1)} custom-call(bf16[2,256,1024]{2,1,0:T(8,128)(2,1)} %act.1, s32[2,512,1]{2,1,0:T(8,128)} %broadcast_select_fusion.slots, bf16[1536,1024]{1,0:T(8,128)(2,1)} %bitcast.7, bf16[8192,3584]{1,0:T(8,128)(2,1)} %gate.1, bf16[1536,3584]{1,0:T(8,128)(2,1)} %bitcast.6), custom_call_target="tpu_custom_call" | custom-call | flops 41339060224 | bytes 83886080 | tf_op jit(solution)/shard_map/pallas_call | solution.py:390
  101.5 4.1 %copy.15 = bf16[2,256,3584]{2,1,0:T(8,128)(2,1)} copy(bf16[2,256,3584]{2,1,0:T(8,128)(2,1)} %shard_map.64) | data formatting | bytes 7340032
  (3 shorter events, 0.0 us)
